TPU v7x, 32 devices: a whole 2x2x4 slice. The times are simulated.
32 devices in a mesh: energy: 8 (over z, y), momentum: 4 (over x, core).
Axes of the slice: x: 2, y: 2, z: 4, core: 2. Of those that a mesh axis runs over, the one named last changes fastest.
Arguments:
- lesser: bfloat16 [8, 4, 2, 512, 512], P('energy', 'momentum'), may hold values from -6 to 6
- greater: bfloat16 [8, 4, 2, 512, 512], P('energy', 'momentum'), may hold values from -6 to 6
- retarded: bfloat16 [8, 4, 2, 512, 512], P('energy', 'momentum'), may hold values from -4.1875 to 4.1875
- occupation: float32 [2], replicated, may hold values from 0.1 to 2
- shift_slots: int32 [2, 2, 8], replicated, may hold values from 0 to 8, as said below
- coupling: int32 [2, 4, 4], replicated, may hold values from 1 to 8
Outputs:
- lesser_new: bfloat16 [8, 4, 2, 512, 512], P('energy', 'momentum')
- greater_new: bfloat16 [8, 4, 2, 512, 512], P('energy', 'momentum')
- retarded_new: bfloat16 [8, 4, 2, 512, 512], P('energy', 'momentum')
Inputs may be any that keep to these rules, and one draw needn't show every extreme that they name: The energies of the grid are held in slots in an order of their own, one energy a slot. Mode m has one shift, the same for all slots: shift_slots[m, 0, j] is the slot of the energy that lies that shift below the energy of slot j, shift_slots[m, 1, j] the slot of the energy as far above it, and 8 where that energy lies outside the grid.
All inputs are finite; a program needn't handle non-finite values.
Results may differ from a plain program's by a relative error of at most 0.0064.
Values may be sent and summed in bfloat16 or wider, within the bound.
A program may use at most 64 MiB of HBM per device.

v0:
```python
import functools

import jax
import jax.numpy as jnp
from jax import lax
from jax.experimental import pallas as pl
from jax.experimental.pallas import tpu as pltpu
from jax.sharding import PartitionSpec as P

MESH = pl.DeviceIdType.MESH


def dot(a, b):
    return jnp.dot(a, b, preferred_element_type=jnp.float32)


def dot_t(a, b):
    return lax.dot_general(a, b, (((1,), (1,)), ((), ())), preferred_element_type=jnp.float32)


def kernel(
    sizes,
    factor,
    less_ref,
    more_ref,
    ret_ref,
    occ_ref,
    shift_ref,
    coup_ref,
    less_out,
    more_out,
    ret_out,
    ret_held,
    occ_held,
    shift_held,
    coup_held,
    recv_less,
    recv_more,
    mixed,
    send_less,
    send_more,
    sig_less,
    sig_more,
    half,
    half_ret,
    half_less,
    sum_more,
    sum_ret,
    send_sem,
    recv_sem,
    own_sem,
    load_sem,
):
    energies, momenta, modes, parts, rows, cols, row_groups, col_groups = sizes
    n = energies * momenta
    my_e, my_m = lax.axis_index("energy"), lax.axis_index("momentum")
    me = my_e * momenta + my_m
    order = row_groups * rows

    pieces = max(cols // 256, 1)
    width = cols // pieces

    my_row = [lax.rem(my_m + m + 1, momenta) for m in range(momenta)]

    def others(act):
        def at_energy(t, carry):
            odd = lax.rem(t, 2)
            half_t = lax.div(t + odd, 2)
            offset = energies // 2 + half_t - 2 * odd * half_t
            e = lax.rem(my_e + offset, energies)
            for m in my_row:
                act(e, m)
            return carry

        lax.fori_loop(0, energies - 1, at_energy, 0)
        for m in my_row[:-1]:
            act(my_e, m)

    def piece(ref, lead, d, begin, count):
        row = pl.multiple_of(lax.rem(d, row_groups) * rows, rows)
        rest = lax.div(d, row_groups)
        col = pl.multiple_of(lax.rem(rest, col_groups) * cols, cols) + begin
        part = lax.div(rest, col_groups) * parts
        index = (pl.ds(part, parts), pl.ds(row, rows), pl.ds(col, count))
        return ref.at[(0,) * lead + index]

    barrier = pltpu.get_barrier_semaphore()

    def greet(e, m):
        pl.semaphore_signal(barrier, inc=1, device_id=(e, m), device_id_type=MESH)

    others(greet)
    loads = [
        pltpu.make_async_copy(piece(less_ref, 2, me, 0, cols), recv_less.at[me], own_sem.at[0]),
        pltpu.make_async_copy(piece(more_ref, 2, me, 0, cols), recv_more.at[me], own_sem.at[1]),
        pltpu.make_async_copy(ret_ref, ret_held, load_sem.at[0]),
        pltpu.make_async_copy(occ_ref, occ_held, load_sem.at[1]),
        pltpu.make_async_copy(shift_ref, shift_held, load_sem.at[2]),
        pltpu.make_async_copy(coup_ref, coup_held, load_sem.at[3]),
    ]
    for load in loads:
        load.start()
    pl.semaphore_wait(barrier, n - 1)

    def forward(ref, landing, which):
        def send(e, m):
            pltpu.make_async_remote_copy(
                src_ref=piece(ref, 2, e * momenta + m, 0, cols),
                dst_ref=landing.at[me],
                send_sem=send_sem.at[which],
                recv_sem=recv_sem.at[which],
                device_id=(e, m),
                device_id_type=MESH,
            ).start()

        others(send)

    def back(ref, landing, begin, count, which):
        def send(e, m):
            pltpu.make_async_remote_copy(
                src_ref=ref.at[e * momenta + m, :, :, pl.ds(begin, count)],
                dst_ref=piece(landing, 0, me, begin, count),
                send_sem=send_sem.at[which],
                recv_sem=recv_sem.at[which],
                device_id=(e, m),
                device_id_type=MESH,
            ).start()

        others(send)

    def wait_all(sem, count):
        span = recv_less.at[pl.ds(0, n - 1), :, :, pl.ds(0, count)]
        pltpu.make_async_copy(span, span, sem).wait()

    forward(less_ref, recv_less, 0)
    forward(more_ref, recv_more, 1)

    mixed[:, energies] = jnp.zeros((modes, momenta, parts, rows, cols), jnp.float32)

    def mix(recv, send, add_below, add_above, begin, count):
        step = min(count, 256)
        blocks = parts * (count // step)

        def place(i):
            b = lax.rem(i, blocks)
            col = begin + lax.rem(b, count // step) * step
            at = pl.ds(pl.multiple_of(col, step), step)
            return lax.div(i, blocks), lax.div(b, count // step), at

        def over_momenta(i, carry):
            s, part, at = place(i)
            terms = [recv[s * momenta + q, part, :, at].astype(jnp.float32) for q in range(momenta)]
            for m in range(modes):
                for k in range(momenta):
                    total = coup_held[m, k, 0].astype(jnp.float32) * terms[0]
                    for q in range(1, momenta):
                        total += coup_held[m, k, q].astype(jnp.float32) * terms[q]
                    mixed[m, s, k, part, :, at] = total
            return carry

        lax.fori_loop(0, energies * blocks, over_momenta, 0)

        def over_energies(i, carry):
            j, part, at = place(i)
            for k in range(momenta):
                total = None
                for m in range(modes):
                    phonons = occ_held[m]
                    for side, add in ((0, add_below), (1, add_above)):
                        term = ((phonons + add) * factor) * mixed[m, shift_held[m, side, j], k, part, :, at]
                        total = term if total is None else total + term
                send[j * momenta + k, part, :, at] = total.astype(jnp.bfloat16)
            return carry

        lax.fori_loop(0, energies * blocks, over_energies, 0)

    for load in loads[2:]:
        load.wait()
    loads[0].wait()
    wait_all(recv_sem.at[0], cols)
    mix(recv_less, send_less, 0.0, 1.0, 0, cols)
    back(send_less, sig_less, 0, cols, 2)
    keep_less = pltpu.make_async_copy(send_less.at[me], piece(sig_less, 0, me, 0, cols), own_sem.at[0])
    keep_less.start()

    loads[1].wait()
    wait_all(recv_sem.at[1], cols)
    keeps = []
    for c in range(pieces):
        begin = c * width
        mix(recv_more, send_more, 1.0, 0.0, begin, width)
        back(send_more, sig_more, begin, width, 3 + c)
        keep = pltpu.make_async_copy(
            send_more.at[me, :, :, pl.ds(begin, width)],
            piece(sig_more, 0, me, begin, width),
            own_sem.at[1 + c],
        )
        keep.start()
        keeps.append(keep)

    ret_re, ret_im = ret_held.at[0, 0, 0], ret_held.at[0, 0, 1]

    def halfway(sigma, at):
        re, im = sigma[0, :, at], sigma[1, :, at]
        left_re, left_im = ret_re[...], ret_im[...]
        return (
            dot(left_re, re) - dot(left_im, im),
            dot(left_re, im) + dot(left_im, re),
        )

    def adjoint(which, at, to):
        re, im = half[0, :, at], half[1, :, at]
        right_re, right_im = ret_re[to, at], ret_im[to, at]
        if which == 0:
            return dot_t(re, right_re) + dot_t(im, right_im)
        return dot_t(im, right_re) - dot_t(re, right_im)

    def dyson(which, at, to):
        re, im = half_ret[0, :, at], half_ret[1, :, at]
        right_re, right_im = ret_re[at, to], ret_im[at, to]
        if which == 0:
            return dot(re, right_re) - dot(im, right_im)
        return dot(re, right_im) + dot(im, right_re)

    tile = min(order, 256)
    tiles = [pl.ds(t * tile, tile) for t in range(order // tile)]

    keep_less.wait()
    wait_all(recv_sem.at[2], cols)
    for at in tiles:
        re, im = halfway(sig_less, at)
        half_less[0, :, at] = re
        half_less[1, :, at] = im
        half[0, :, at] = re.astype(jnp.bfloat16)
        half[1, :, at] = im.astype(jnp.bfloat16)
    for to in tiles:
        for x in range(2):
            less_out[0, 0, x, :, to] = adjoint(x, pl.ds(0, order), to).astype(jnp.bfloat16)

    stages = pieces if col_groups == 1 else 1
    span = order // stages
    for c in range(pieces):
        keeps[c].wait()
        wait_all(recv_sem.at[3 + c], width)
        if stages == 1 and c < pieces - 1:
            continue
        stage = c if stages > 1 else 0
        last = stage == stages - 1
        for t in range(span // tile):
            at = pl.ds(stage * span + t * tile, tile)
            for x, value in enumerate(halfway(sig_more, at)):
                half[x, :, at] = value.astype(jnp.bfloat16)
                half_ret[x, :, at] = ((value - half_less[x, :, at]) * 0.5).astype(jnp.bfloat16)
        at = pl.ds(stage * span, span)
        for to in tiles:
            for x in range(2):
                more, ret = adjoint(x, at, to), dyson(x, at, to)
                if stage > 0:
                    more += sum_more[x, :, to]
                    ret += sum_ret[x, :, to]
                if last:
                    more_out[0, 0, x, :, to] = more.astype(jnp.bfloat16)
                    ret += (ret_re, ret_im)[x][:, to].astype(jnp.float32)
                    ret_out[0, 0, x, :, to] = ret.astype(jnp.bfloat16)
                else:
                    sum_more[x, :, to] = more
                    sum_ret[x, :, to] = ret
    for which in range(3):
        wait_all(send_sem.at[which], cols)
    for c in range(pieces):
        wait_all(send_sem.at[3 + c], width)


def per_device(energies, momenta, lesser, greater, retarded, occupation, shift_slots, coupling):
    n = energies * momenta
    modes = coupling.shape[0]
    order = lesser.shape[-1]
    factor = 1.0 / (order * 4.0 * (modes * momenta) ** 0.5)
    row_groups = min(n, order // 16)
    col_groups = min(n // row_groups, order // 128)
    part_groups = n // (row_groups * col_groups)
    parts, rows, cols = 2 // part_groups, order // row_groups, order // col_groups
    sizes = (energies, momenta, modes, parts, rows, cols, row_groups, col_groups)
    vmem = pl.BlockSpec(memory_space=pltpu.VMEM)
    hbm = pl.BlockSpec(memory_space=pltpu.HBM)
    pieces = max(cols // 256, 1)
    exchanged = pltpu.VMEM((n, parts, rows, cols), jnp.bfloat16)
    block = pltpu.VMEM((2, order, order), jnp.bfloat16)
    wide = pltpu.VMEM((2, order, order), jnp.float32)
    return pl.pallas_call(
        functools.partial(kernel, sizes, factor),
        out_shape=tuple(jax.ShapeDtypeStruct(lesser.shape, jnp.bfloat16) for _ in range(3)),
        in_specs=[hbm] * 6,
        out_specs=(vmem, vmem, vmem),
        scratch_shapes=[
            pltpu.VMEM(retarded.shape, jnp.bfloat16),
            pltpu.SMEM(occupation.shape, jnp.float32),
            pltpu.SMEM(shift_slots.shape, jnp.int32),
            pltpu.SMEM(coupling.shape, jnp.int32),
            exchanged,
            exchanged,
            pltpu.VMEM((modes, energies + 1, momenta, parts, rows, cols), jnp.float32),
            exchanged,
            exchanged,
            block,
            block,
            block,
            block,
            wide,
            wide,
            wide,
            pltpu.SemaphoreType.DMA((3 + pieces,)),
            pltpu.SemaphoreType.DMA((3 + pieces,)),
            pltpu.SemaphoreType.DMA((1 + pieces,)),
            pltpu.SemaphoreType.DMA((4,)),
        ],
        compiler_params=pltpu.CompilerParams(
            collective_id=0, has_side_effects=True, vmem_limit_bytes=50 * 1024 * 1024
        ),
        cost_estimate=pl.CostEstimate(
            flops=48 * order**3, bytes_accessed=24 * order * order, transcendentals=0
        ),
    )(lesser, greater, retarded, occupation, shift_slots, coupling)


def solution(mesh):
    split = P("energy", "momentum", None, None, None)
    return jax.shard_map(
        functools.partial(per_device, mesh.shape["energy"], mesh.shape["momentum"]),
        mesh=mesh,
        in_specs=(split, split, split, P(), P(), P()),
        out_specs=(split, split, split),
        check_vma=False,
    )
```

profile of v0, /device:TPU:9, one launch (start us, length us, event | category | flops | bytes accessed | tf_op | source)
XLA Modules:
  0.0 103.0 jit_solution(4627601855361613323)
XLA Ops:
  0.6 0.0 copy-start
  0.6 0.7 copy-done
  1.3 0.0 copy-start.1
  1.3 0.7 copy-done.1
  2.0 0.0 copy-start.2
  2.0 0.7 copy-done.2
  2.7 97.4 %shard_map.85 = (bf16[1,1,2,512,512]{4,3,2,1,0:T(8,128)(2,1)S(1)}, bf16[1,1,2,512,512]{4,3,2,1,0:T(8,128)(2,1)S(1)}, bf16[1,1,2,512,512]{4,3,2,1,0:T(8,128)(2,1)S(1)}) custom-call(bf16[1,1,2,512,512]{4,3,2,1,0:T(8,128)(2,1)} %less_ref.1, bf16[1,1,2,512,512]{4,3,2,1,0:T(8,128)(2,1)} %more_ref.1, bf16[1,1,2,512,512]{4,3,2,1,0:T(8,128)(2,1)} %ret_ref.1, ...), custom_call_target="tpu_custom_call" | custom-call | flops 6442450944 | bytes 6291456 | tf_op jit(solution)/shard_map/pallas_call | solution.py:290
  100.1 1.0 copy.12
  101.1 1.0 copy.13
  102.0 1.0 copy.14
Async XLA Ops:
  0.6 0.7 copy-start
  1.3 0.7 copy-start.1
  2.0 0.7 copy-start.2
where the time goes:
time: 104 us; the launch traced here: 103 us
  Pallas kernels  97.4 us (94%)
  local copies, waits for them, and re-layouts  4.93 us (5%)
    pallas_call x1, Pallas kernels, per_device(): pl.pallas_call(functools.partial(kernel, sizes, factor), out_shape=tuple(...  97.4 us
    unnamed x9, local copies, waits for them, and re-layouts  4.93 us

commit v1 on v0

v1 whole, which is shorter than its diff:
```python
import functools

import jax
import jax.numpy as jnp
from jax import lax
from jax.experimental import pallas as pl
from jax.experimental.pallas import tpu as pltpu
from jax.sharding import PartitionSpec as P

MESH = pl.DeviceIdType.MESH
STEP = 128
GRAIN = 2.0**27


def dot(a, b):
    return jnp.dot(a, b, preferred_element_type=jnp.float32)


def dot_t(a, b):
    return lax.dot_general(a, b, (((1,), (1,)), ((), ())), preferred_element_type=jnp.float32)


def products(ret, sigma, at, half_less, less_at, width):
    both = jnp.concatenate([sigma[0, :, at], sigma[1, :, at]], axis=1)
    by_re, by_im = dot(ret[0], both), dot(ret[1], both)
    more = by_re[:, :width] - by_im[:, width:], by_re[:, width:] + by_im[:, :width]
    wide = tuple((more[x] - half_less[x, :, less_at]) * 0.5 for x in range(2))
    return tuple(v.astype(jnp.bfloat16) for v in more), tuple(v.astype(jnp.bfloat16) for v in wide)


def adjoint_part(ret, half, at, to):
    re, im = half
    right = jnp.concatenate([ret[0, to, at], ret[1, to, at]], axis=1)
    return (
        dot_t(jnp.concatenate([re, im], axis=1), right),
        dot_t(jnp.concatenate([im, -re], axis=1), right),
    )


def dyson_part(ret, half, at, to):
    re, im = half
    right_re, right_im = ret[0, at, to], ret[1, at, to]
    return (
        dot(jnp.concatenate([re, -im], axis=1), jnp.concatenate([right_re, right_im], axis=0)),
        dot(jnp.concatenate([re, im], axis=1), jnp.concatenate([right_im, right_re], axis=0)),
    )


def kernel(sizes, factor, widths, tail, less_ref, more_ref, ret_ref, small_ref, *refs):
    energies, momenta, modes, parts, rows, cols, row_groups, col_groups = sizes
    stages = len(widths)
    less_new, ret_held, tail_less, tail_more, *refs = refs
    sum_more, sum_ret, refs = refs[:2], refs[2:4], refs[4:]
    small, recv_less, recv_more, mixed, send_less, sig_less, half, half_less, *refs = refs
    send_more, refs = refs[:stages], refs[stages:]
    sig_more, refs = refs[: stages - 1] + [tail_more], refs[stages - 1 :]
    send_sem, recv_sem, own_sem, load_sem, ready_sem = refs
    n = energies * momenta
    me = lax.axis_index("energy") * momenta + lax.axis_index("momentum")
    order = row_groups * rows
    bits = n.bit_length() - 1
    mine = [lax.rem(lax.div(me, 1 << b), 2) for b in range(bits)]

    def partner(d):
        other = 0
        for b in range(bits):
            flip = (d >> b) % 2 if isinstance(d, int) else lax.rem(lax.div(d, 1 << b), 2)
            other += (mine[b] + flip - 2 * mine[b] * flip) * (1 << b)
        return other

    def place(d):
        return lax.div(d, momenta), lax.rem(d, momenta)

    quarter = n // 4
    low = quarter.bit_length() - 1
    my_quarter = lax.div(me, quarter)
    my_half = lax.div(my_quarter, 2)
    far_half = 2 * (1 - my_half)
    near_quarter = 4 * my_half + 1 - my_quarter

    def others(act):
        def within(q, last):
            def at(t, carry):
                other = q * quarter
                for b in range(low):
                    flip = lax.rem(lax.div(quarter - 1 - t, 1 << b), 2)
                    other += (mine[b] + flip - 2 * mine[b] * flip) * (1 << b)
                act(other)
                return carry

            lax.fori_loop(0, last, at, 0)

        within(far_half, quarter)
        within(near_quarter, quarter)
        within(far_half + 1, quarter)
        within(my_quarter, quarter - 1)

    def piece(ref, lead, d, count):
        row = pl.multiple_of(lax.rem(d, row_groups) * rows, rows)
        rest = lax.div(d, row_groups)
        col = pl.multiple_of(lax.rem(rest, col_groups) * count, count)
        part = lax.div(rest, col_groups) * parts
        index = (pl.ds(part, parts), pl.ds(row, rows), pl.ds(col, count))
        return ref.at[(0,) * lead + index]

    def signal(sem, d):
        pl.semaphore_signal(sem, inc=1, device_id=place(d), device_id_type=MESH)

    barrier = pltpu.get_barrier_semaphore()
    for b in range(bits):
        signal(barrier, partner(1 << b))
    loads = [
        pltpu.make_async_copy(piece(less_ref, 2, me, cols), recv_less.at[me], own_sem.at[0]),
        pltpu.make_async_copy(piece(more_ref, 2, me, cols), recv_more.at[me], own_sem.at[1]),
        pltpu.make_async_copy(ret_ref.at[0, 0], ret_held, load_sem.at[0]),
        pltpu.make_async_copy(small_ref, small, load_sem.at[1]),
    ]
    for load in loads:
        load.start()

    def forward(ref, landing, which):
        def send(d):
            pltpu.make_async_remote_copy(
                src_ref=piece(ref, 2, d, cols),
                dst_ref=landing.at[me],
                send_sem=send_sem.at[which],
                recv_sem=recv_sem.at[which],
                device_id=place(d),
                device_id_type=MESH,
            ).start()

        return send

    def back(ref, landing, count, which):
        def send(d):
            pltpu.make_async_remote_copy(
                src_ref=ref.at[d],
                dst_ref=piece(landing, 0, me, count),
                send_sem=send_sem.at[which],
                recv_sem=recv_sem.at[which],
                device_id=place(d),
                device_id_type=MESH,
            ).start()

        others(send)

    def wait_all(sem, ref):
        span = ref.at[pl.ds(0, n - 1)]
        pltpu.make_async_copy(span, span, sem).wait()

    send = forward(less_ref, recv_less, 0)
    for level in range(bits):
        if level == 0:
            pl.semaphore_wait(barrier, bits)
        else:
            pl.semaphore_wait(ready_sem.at[level - 1], bits)
        if level < bits - 1:
            for b in range(bits):
                signal(ready_sem.at[level], partner(1 << b))
        for d in range(n - 1, 0, -1):
            if d.bit_count() == level + 1:
                send(partner(d))
    others(forward(more_ref, recv_more, 1))

    mixed[:, energies] = jnp.zeros((modes, momenta, parts, rows, cols), jnp.float32)

    def coupling(m, k, q):
        return small[m, k, q].astype(jnp.float32)

    def mix(recv, send, add_below, add_above, begin, count):
        step = min(count, max(4096 // rows, 128))
        blocks = parts * (count // step)

        def spot(i):
            b = lax.rem(i, blocks)
            col = lax.rem(b, count // step) * step
            return lax.div(i, blocks), lax.div(b, count // step), pl.multiple_of(col, step)

        def over_momenta(i, carry):
            s, part, col = spot(i)
            at = pl.ds(begin + col, step)
            terms = [recv[s * momenta + q, part, :, at].astype(jnp.float32) for q in range(momenta)]
            for m in range(modes):
                for k in range(momenta):
                    total = coupling(m, k, 0) * terms[0]
                    for q in range(1, momenta):
                        total += coupling(m, k, q) * terms[q]
                    mixed[m, s, k, part, :, at] = total
            return carry

        lax.fori_loop(0, energies * blocks, over_momenta, 0)

        def over_energies(i, carry):
            j, part, col = spot(i)
            at, to = pl.ds(begin + col, step), pl.ds(col, step)
            for k in range(momenta):
                total = None
                for m in range(modes):
                    phonons = small[m, momenta + 2, 0].astype(jnp.float32) * (1.0 / GRAIN)
                    for side, add in ((0, add_below), (1, add_above)):
                        slot = small[m, momenta + side, j]
                        term = ((phonons + add) * factor) * mixed[m, slot, k, part, :, at]
                        total = term if total is None else total + term
                send[j * momenta + k, part, :, to] = total.astype(jnp.bfloat16)
            return carry

        lax.fori_loop(0, energies * blocks, over_energies, 0)

    loads[3].wait()
    loads[0].wait()
    wait_all(recv_sem.at[0], recv_less)
    mix(recv_less, send_less, 0.0, 1.0, 0, cols)
    back(send_less, sig_less, cols, 2)
    keep_less = pltpu.make_async_copy(send_less.at[me], piece(sig_less, 0, me, cols), own_sem.at[0])
    keep_less.start()

    loads[1].wait()
    wait_all(recv_sem.at[1], recv_more)
    keeps, begin = [], 0
    for c, width in enumerate(widths):
        mix(recv_more, send_more[c], 1.0, 0.0, begin, width)
        back(send_more[c], sig_more[c], width, 3 + c)
        keep = pltpu.make_async_copy(send_more[c].at[me], piece(sig_more[c], 0, me, width), own_sem.at[1 + c])
        keep.start()
        keeps.append(keep)
        begin += width

    tile = min(order, 256)
    tiles = [pl.ds(t * tile, tile) for t in range(order // tile)]

    loads[2].wait()
    keep_less.wait()
    wait_all(recv_sem.at[2], send_less)
    for at in tiles:
        both_re, both_im = sig_less[0, :, at], sig_less[1, :, at]
        re = dot(ret_held[0], both_re) - dot(ret_held[1], both_im)
        im = dot(ret_held[0], both_im) + dot(ret_held[1], both_re)
        for x, value in enumerate((re, im)):
            half_less[x, :, at] = value
            half[x, :, at] = value.astype(jnp.bfloat16)
    tail_less[...] = half_less[:, :, tail:]
    for to in tiles:
        re, im, right_re, right_im = half[0], half[1], ret_held[0, to, :], ret_held[1, to, :]
        less_new[0, 0, 0, :, to] = (dot_t(re, right_re) + dot_t(im, right_im)).astype(jnp.bfloat16)
        less_new[0, 0, 1, :, to] = (dot_t(im, right_re) - dot_t(re, right_im)).astype(jnp.bfloat16)
    for x in range(2):
        for to in tiles:
            sum_ret[x][:, to] = ret_held[x, :, to].astype(jnp.float32)
            if tail == 0:
                sum_more[x][:, to] = jnp.zeros((order, tile), jnp.float32)

    begin = 0
    for c, width in enumerate(widths):
        keeps[c].wait()
        wait_all(recv_sem.at[3 + c], send_more[c])
        if begin < tail:
            for part in range(width // STEP):
                at = pl.ds(begin + part * STEP, STEP)
                more, wide = products(ret_held, sig_more[c], pl.ds(part * STEP, STEP), half_less, at, STEP)
                for to in tiles:
                    add_more, add_ret = adjoint_part(ret_held, more, at, to), dyson_part(ret_held, wide, at, to)
                    for x in range(2):
                        sum_ret[x][:, to] += add_ret[x]
                        if begin + part == 0:
                            sum_more[x][:, to] = add_more[x]
                        else:
                            sum_more[x][:, to] += add_more[x]
        begin += width
    for which, ref in enumerate([recv_less, recv_more, send_less, *send_more]):
        wait_all(send_sem.at[which], ref)


def finish(tail, less_new, ret_held, tail_less, tail_more, *refs):
    sum_more, sum_ret, refs = refs[:2], refs[2:4], refs[4:]
    less_out, more_out, ret_out, more_new, ret_new, sem = refs
    order = less_new.shape[-1]
    copies = [pltpu.make_async_copy(less_new, less_out, sem.at[0])]
    copies[0].start()
    tile = min(order, 256)
    steps = range(tail, order, STEP)
    halves = []
    for b in steps:
        at = pl.ds(b - tail, STEP)
        halves.append(products(ret_held, tail_more, at, tail_less, at, STEP))
    for t in range(order // tile):
        to = pl.ds(t * tile, tile)
        more, ret = [sum_more[x][:, to] for x in range(2)], [sum_ret[x][:, to] for x in range(2)]
        for b, (half_more, half_ret) in zip(steps, halves):
            add_more = adjoint_part(ret_held, half_more, pl.ds(b, STEP), to)
            add_ret = dyson_part(ret_held, half_ret, pl.ds(b, STEP), to)
            more = [more[x] + add_more[x] for x in range(2)]
            ret = [ret[x] + add_ret[x] for x in range(2)]
        for x in range(2):
            more_new[x, :, to] = more[x].astype(jnp.bfloat16)
            ret_new[x, :, to] = ret[x].astype(jnp.bfloat16)
        for i, (made, out) in enumerate(((more_new, more_out), (ret_new, ret_out))):
            copy = pltpu.make_async_copy(made.at[:, :, to], out.at[0, 0, :, :, to], sem.at[1 + 2 * t + i])
            copy.start()
            copies.append(copy)
    for copy in copies:
        copy.wait()


def per_device(energies, momenta, lesser, greater, retarded, occupation, shift_slots, coupling):
    n = energies * momenta
    modes = coupling.shape[0]
    order = lesser.shape[-1]
    factor = 1.0 / (order * 4.0 * (modes * momenta) ** 0.5)
    row_groups = min(n // 2, order // 16)
    col_groups = n // 2 // row_groups
    parts, rows, cols = 1, order // row_groups, order // col_groups
    sizes = (energies, momenta, modes, parts, rows, cols, row_groups, col_groups)
    vmem = pl.BlockSpec(memory_space=pltpu.VMEM)
    hbm = pl.BlockSpec(memory_space=pltpu.HBM)
    widths = (384, 128) if cols == 512 else (cols,)
    tail = order - widths[-1] if col_groups == 1 else 0
    stages = len(widths)

    def exchanged(width):
        return pltpu.VMEM((n, parts, rows, width), jnp.bfloat16)

    whole = pltpu.VMEM((2, order, order), jnp.bfloat16)
    new = jax.ShapeDtypeStruct(lesser.shape, jnp.bfloat16)
    total = jax.ShapeDtypeStruct((order, order), jnp.float32)
    length = max(energies, momenta)
    small = jnp.concatenate(
        [
            jnp.pad(coupling, ((0, 0), (0, 0), (0, length - momenta))),
            jnp.pad(shift_slots, ((0, 0), (0, 0), (0, length - energies))),
            jnp.broadcast_to((occupation * GRAIN).astype(jnp.int32)[:, None, None], (modes, 1, length)),
        ],
        axis=1,
    )
    held = pl.pallas_call(
        functools.partial(kernel, sizes, factor, widths, tail),
        out_shape=(
            new,
            jax.ShapeDtypeStruct((2, order, order), jnp.bfloat16),
            jax.ShapeDtypeStruct((2, order, order - tail), jnp.float32),
            jax.ShapeDtypeStruct((2, order, order - tail), jnp.bfloat16),
            *[total] * 4,
        ),
        in_specs=[hbm] * 4,
        out_specs=(vmem,) * 8,
        scratch_shapes=[
            pltpu.SMEM(small.shape, jnp.int32),
            exchanged(cols),
            exchanged(cols),
            pltpu.VMEM((modes, energies + 1, momenta, parts, rows, cols), jnp.float32),
            exchanged(cols),
            whole,
            whole,
            pltpu.VMEM((2, order, order), jnp.float32),
            *[exchanged(width) for width in widths],
            *[pltpu.VMEM((2, order, width * col_groups), jnp.bfloat16) for width in widths[:-1]],
            pltpu.SemaphoreType.DMA((3 + stages,)),
            pltpu.SemaphoreType.DMA((3 + stages,)),
            pltpu.SemaphoreType.DMA((1 + stages,)),
            pltpu.SemaphoreType.DMA((2,)),
            pltpu.SemaphoreType.REGULAR((n.bit_length() - 2,)),
        ],
        compiler_params=pltpu.CompilerParams(
            collective_id=0, has_side_effects=True, vmem_limit_bytes=47 * 1024 * 1024
        ),
        cost_estimate=pl.CostEstimate(
            flops=40 * order**3, bytes_accessed=24 * order * order, transcendentals=0
        ),
    )(lesser, greater, retarded, small)
    return pl.pallas_call(
        functools.partial(finish, tail),
        out_shape=(new, new, new),
        in_specs=[vmem] * 8,
        out_specs=(hbm,) * 3,
        scratch_shapes=[
            whole,
            whole,
            pltpu.SemaphoreType.DMA((1 + 2 * max(order // 256, 1),)),
        ],
        compiler_params=pltpu.CompilerParams(vmem_limit_bytes=16 * 1024 * 1024),
        cost_estimate=pl.CostEstimate(
            flops=8 * order**3, bytes_accessed=12 * order * order, transcendentals=0
        ),
    )(*held)


def solution(mesh):
    split = P("energy", "momentum", None, None, None)
    return jax.shard_map(
        functools.partial(per_device, mesh.shape["energy"], mesh.shape["momentum"]),
        mesh=mesh,
        in_specs=(split, split, split, P(), P(), P()),
        out_specs=(split, split, split),
        check_vma=False,
    )
```

time: 104 us -> 101 us (0.971)
  local copies, waits for them, and re-layouts: 4.93 us -> 0.08 us
  other arithmetic: 0 us -> 1.36 us
    unnamed x9 -> x2, local copies, waits for them, and re-layouts: 4.93 us -> 0.01 us
    pallas_call x1 -> x2, Pallas kernels: 97.4 us -> 97.3 us  [the longest x1 95.4 us: per_device(): pl.pallas_call(functools.partial(kernel, sizes, factor, widths, tail), ou...]
where the time goes in v1:
time: 101 us; the launch traced here: 99.4 us
  Pallas kernels  97.3 us (96%)
  other arithmetic  1.36 us (1%)
    pallas_call x1, Pallas kernels, per_device(): pl.pallas_call(functools.partial(kernel, sizes, factor, widths, tail), ou...  95.4 us

profile of v1, /device:TPU:9, one launch (start us, length us, event | category | flops | bytes accessed | tf_op | source)
XLA Modules:
  0.0 99.4 jit_solution(12578716478194591354)
XLA Ops:
  0.6 0.0 copy-start
  0.6 0.7 multiply_convert_fusion
  1.3 0.1 broadcast_in_dim.2
  1.4 0.0 copy-done
  1.4 0.7 fusion.small_ref
  2.1 95.4 %shard_map.85 = (bf16[1,1,2,512,512]{4,3,2,1,0:T(8,128)(2,1)S(1)}, bf16[2,512,512]{2,1,0:T(8,128)(2,1)S(1)}, f32[2,512,128]{2,1,0:T(8,128)S(1)}, bf16[2,512,128]...) custom-call(bf16[1,1,2,512,512]{4,3,2,1,0:T(8,128)(2,1)} %less_ref.1, ...), custom_call_target="tpu_custom_call" | custom-call | flops 5368709120 | bytes 6291456 | tf_op jit(solution)/shard_map/pallas_call | solution.py:334
  97.5 1.9 %shard_map.86 = (bf16[1,1,2,512,512]{4,3,2,1,0:T(8,128)(2,1)}, bf16[1,1,2,512,512]{4,3,2,1,0:T(8,128)(2,1)}, bf16[1,1,2,512,512]{4,3,2,1,0:T(8,128)(2,1)}) custom-call(bf16[1,1,2,512,512]{4,3,2,1,0:T(8,128)(2,1)S(1)} %get-tuple-element.11.less_new, bf16[2,512,512]{2,1,0:T(8,128)(2,1)S(1)} %get-tuple-element.12.ret_held, ...), custom_call_target="tpu_custom_call" | custom-call | flops 1073741824 | bytes 3145728 | tf_op jit(solution)/shard_map/pallas_call | solution.py:369
Async XLA Ops:
  0.6 0.8 copy-start

commit v2 on v1

--- a/solution.py
+++ b/solution.py
@@ -78,22 +78,38 @@
     far_half = 2 * (1 - my_half)
     near_quarter = 4 * my_half + 1 - my_quarter
 
-    def others(act):
-        def within(q, last):
+    def others(act, ending=False):
+        def target(q, t, fixed):
+            if fixed:
+                return q * quarter + t
+            other = q * quarter
+            for b in range(low):
+                flip = lax.rem(lax.div(quarter - 1 - t, 1 << b), 2)
+                other += (mine[b] + flip - 2 * mine[b] * flip) * (1 << b)
+            return other
+
+        def blend(quarters, fixed):
             def at(t, carry):
-                other = q * quarter
-                for b in range(low):
-                    flip = lax.rem(lax.div(quarter - 1 - t, 1 << b), 2)
-                    other += (mine[b] + flip - 2 * mine[b] * flip) * (1 << b)
-                act(other)
+                for q in quarters:
+                    act(target(q, t, fixed))
                 return carry
 
-            lax.fori_loop(0, last, at, 0)
-
-        within(far_half, quarter)
-        within(near_quarter, quarter)
-        within(far_half + 1, quarter)
-        within(my_quarter, quarter - 1)
+            lax.fori_loop(0, quarter, at, 0)
+
+        def own(t, carry):
+            act(target(my_quarter, t, False))
+            return carry
+
+        if ending:
+            blend([far_half], True)
+            blend([near_quarter], True)
+            blend([far_half + 1], True)
+            lax.fori_loop(0, quarter - 1, own, 0)
+        else:
+            blend([far_half], False)
+            blend([near_quarter], False)
+            blend([far_half + 1], False)
+            lax.fori_loop(0, quarter - 1, own, 0)
 
     def piece(ref, lead, d, count):
         row = pl.multiple_of(lax.rem(d, row_groups) * rows, rows)
@@ -131,7 +147,7 @@
 
         return send
 
-    def back(ref, landing, count, which):
+    def back(ref, landing, count, which, ending=False):
         def send(d):
             pltpu.make_async_remote_copy(
                 src_ref=ref.at[d],
@@ -142,7 +158,7 @@
                 device_id_type=MESH,
             ).start()
 
-        others(send)
+        others(send, ending)
 
     def wait_all(sem, ref):
         span = ref.at[pl.ds(0, n - 1)]
@@ -219,7 +235,7 @@
     keeps, begin = [], 0
     for c, width in enumerate(widths):
         mix(recv_more, send_more[c], 1.0, 0.0, begin, width)
-        back(send_more[c], sig_more[c], width, 3 + c)
+        back(send_more[c], sig_more[c], width, 3 + c, c == stages - 1)
         keep = pltpu.make_async_copy(send_more[c].at[me], piece(sig_more[c], 0, me, width), own_sem.at[1 + c])
         keep.start()
         keeps.append(keep)
@@ -323,14 +339,12 @@
     new = jax.ShapeDtypeStruct(lesser.shape, jnp.bfloat16)
     total = jax.ShapeDtypeStruct((order, order), jnp.float32)
     length = max(energies, momenta)
-    small = jnp.concatenate(
-        [
-            jnp.pad(coupling, ((0, 0), (0, 0), (0, length - momenta))),
-            jnp.pad(shift_slots, ((0, 0), (0, 0), (0, length - energies))),
-            jnp.broadcast_to((occupation * GRAIN).astype(jnp.int32)[:, None, None], (modes, 1, length)),
-        ],
-        axis=1,
-    )
+    packed = (modes, momenta + 3, length)
+    row = lax.broadcasted_iota(jnp.int32, packed, 1)
+    grains = (lax.broadcast_in_dim(occupation, packed, (0,)) * GRAIN).astype(jnp.int32)
+    weights = lax.pad(coupling, 0, ((0, 0, 0), (0, 3, 0), (0, length - momenta, 0)))
+    slots = lax.pad(shift_slots, 0, ((0, 0, 0), (momenta, 1, 0), (0, length - energies, 0)))
+    small = jnp.where(row == momenta + 2, grains, weights + slots)
     held = pl.pallas_call(
         functools.partial(kernel, sizes, factor, widths, tail),
         out_shape=(

time: 101 us -> 100 us (0.990)
  no operation moved by 1% of the time
where the time goes in v2:
time: 100 us; the launch traced here: 99.3 us
  Pallas kernels  97.2 us (97%)
  other arithmetic  1.43 us (1%)
    pallas_call x1, Pallas kernels, per_device(): pl.pallas_call(functools.partial(kernel, sizes, factor, widths, tail), ou...  95.3 us

profile of v2, /device:TPU:9, one launch (start us, length us, event | category | flops | bytes accessed | tf_op | source)
XLA Modules:
  0.0 99.3 jit_solution(13127047490460363530)
XLA Ops:
  0.6 0.0 copy-start
  0.6 0.7 multiply_convert_fusion
  1.3 0.0 copy-done
  1.3 0.8 add_select_fusion.small_ref
  2.1 95.3 %shard_map.85 = (bf16[1,1,2,512,512]{4,3,2,1,0:T(8,128)(2,1)S(1)}, bf16[2,512,512]{2,1,0:T(8,128)(2,1)S(1)}, f32[2,512,128]{2,1,0:T(8,128)S(1)}, bf16[2,512,128]...) custom-call(bf16[1,1,2,512,512]{4,3,2,1,0:T(8,128)(2,1)} %less_ref.1, ...), custom_call_target="tpu_custom_call" | custom-call | flops 5368709120 | bytes 6291456 | tf_op jit(solution)/shard_map/pallas_call | solution.py:348
  97.4 1.9 %shard_map.86 = (bf16[1,1,2,512,512]{4,3,2,1,0:T(8,128)(2,1)}, bf16[1,1,2,512,512]{4,3,2,1,0:T(8,128)(2,1)}, bf16[1,1,2,512,512]{4,3,2,1,0:T(8,128)(2,1)}) custom-call(bf16[1,1,2,512,512]{4,3,2,1,0:T(8,128)(2,1)S(1)} %get-tuple-element.11.less_new, bf16[2,512,512]{2,1,0:T(8,128)(2,1)S(1)} %get-tuple-element.12.ret_held, ...), custom_call_target="tpu_custom_call" | custom-call | flops 1073741824 | bytes 3145728 | tf_op jit(solution)/shard_map/pallas_call | solution.py:383
  (1 shorter events, 0.0 us)
Async XLA Ops:
  0.6 0.7 copy-start

commit v3 on v2

--- a/solution.py
+++ b/solution.py
@@ -78,7 +78,7 @@
     far_half = 2 * (1 - my_half)
     near_quarter = 4 * my_half + 1 - my_quarter
 
-    def others(act, ending=False):
+    def others(act, ending=False, first=True, which=("low", "high")):
         def target(q, t, fixed):
             if fixed:
                 return q * quarter + t
@@ -88,27 +88,26 @@
                 other += (mine[b] + flip - 2 * mine[b] * flip) * (1 << b)
             return other
 
-        def blend(quarters, fixed):
+        def blend(quarters, fixed, skip=0):
             def at(t, carry):
                 for q in quarters:
                     act(target(q, t, fixed))
                 return carry
 
-            lax.fori_loop(0, quarter, at, 0)
+            lax.fori_loop(0, quarter - skip, at, 0)
 
         def own(t, carry):
             act(target(my_quarter, t, False))
             return carry
 
-        if ending:
-            blend([far_half], True)
-            blend([near_quarter], True)
-            blend([far_half + 1], True)
-            lax.fori_loop(0, quarter - 1, own, 0)
-        else:
-            blend([far_half], False)
-            blend([near_quarter], False)
-            blend([far_half + 1], False)
+        skip = 0 if first else 1
+        if skip:
+            act((far_half + 1 - lax.rem(my_quarter, 2)) * quarter + lax.rem(me, quarter))
+        if "low" in which:
+            blend([far_half], ending, skip)
+            blend([near_quarter], ending)
+        if "high" in which:
+            blend([far_half + 1], ending, skip)
             lax.fori_loop(0, quarter - 1, own, 0)
 
     def piece(ref, lead, d, count):
@@ -147,7 +146,7 @@
 
         return send
 
-    def back(ref, landing, count, which, ending=False):
+    def back(ref, landing, count, which, ending=False, targets=("low", "high")):
         def send(d):
             pltpu.make_async_remote_copy(
                 src_ref=ref.at[d],
@@ -158,13 +157,14 @@
                 device_id_type=MESH,
             ).start()
 
-        others(send, ending)
+        others(send, ending, which=targets)
 
     def wait_all(sem, ref):
         span = ref.at[pl.ds(0, n - 1)]
         pltpu.make_async_copy(span, span, sem).wait()
 
     send = forward(less_ref, recv_less, 0)
+    send_more_forward = forward(more_ref, recv_more, 1)
     for level in range(bits):
         if level == 0:
             pl.semaphore_wait(barrier, bits)
@@ -176,7 +176,9 @@
         for d in range(n - 1, 0, -1):
             if d.bit_count() == level + 1:
                 send(partner(d))
-    others(forward(more_ref, recv_more, 1))
+                if d == n // 2:
+                    send_more_forward(partner(d))
+    others(send_more_forward, first=False)
 
     mixed[:, energies] = jnp.zeros((modes, momenta, parts, rows, cols), jnp.float32)
 
@@ -235,11 +237,13 @@
     keeps, begin = [], 0
     for c, width in enumerate(widths):
         mix(recv_more, send_more[c], 1.0, 0.0, begin, width)
-        back(send_more[c], sig_more[c], width, 3 + c, c == stages - 1)
+        back(send_more[c], sig_more[c], width, 3 + c, c == stages - 1, ("low",))
         keep = pltpu.make_async_copy(send_more[c].at[me], piece(sig_more[c], 0, me, width), own_sem.at[1 + c])
         keep.start()
         keeps.append(keep)
         begin += width
+    for c, width in enumerate(widths):
+        back(send_more[c], sig_more[c], width, 3 + c, c == stages - 1, ("high",))
 
     tile = min(order, 256)
     tiles = [pl.ds(t * tile, tile) for t in range(order // tile)]
@@ -328,7 +332,7 @@
     sizes = (energies, momenta, modes, parts, rows, cols, row_groups, col_groups)
     vmem = pl.BlockSpec(memory_space=pltpu.VMEM)
     hbm = pl.BlockSpec(memory_space=pltpu.HBM)
-    widths = (384, 128) if cols == 512 else (cols,)
+    widths = (128, 128, 128, 128) if cols == 512 else (cols,)
     tail = order - widths[-1] if col_groups == 1 else 0
     stages = len(widths)
 

time: 100 us -> 99.7 us (level)
  no operation moved by 1% of the time
where the time goes in v3:
time: 99.7 us; the launch traced here: 99.5 us
  Pallas kernels  97.4 us (98%)
  other arithmetic  1.43 us (1%)
    pallas_call x1, Pallas kernels, per_device(): pl.pallas_call(functools.partial(kernel, sizes, factor, widths, tail), ou...  95.5 us

profile of v3, /device:TPU:9, one launch (start us, length us, event | category | flops | bytes accessed | tf_op | source)
XLA Modules:
  0.0 99.5 jit_solution(4003948418830106316)
XLA Ops:
  0.6 0.0 copy-start
  0.6 0.7 multiply_convert_fusion
  1.3 0.0 copy-done
  1.3 0.8 add_select_fusion.small_ref
  2.1 95.5 %shard_map.85 = (bf16[1,1,2,512,512]{4,3,2,1,0:T(8,128)(2,1)S(1)}, bf16[2,512,512]{2,1,0:T(8,128)(2,1)S(1)}, f32[2,512,128]{2,1,0:T(8,128)S(1)}, bf16[2,512,128]...) custom-call(bf16[1,1,2,512,512]{4,3,2,1,0:T(8,128)(2,1)} %less_ref.1, ...), custom_call_target="tpu_custom_call" | custom-call | flops 5368709120 | bytes 6291456 | tf_op jit(solution)/shard_map/pallas_call | solution.py:352
  97.5 1.9 %shard_map.86 = (bf16[1,1,2,512,512]{4,3,2,1,0:T(8,128)(2,1)}, bf16[1,1,2,512,512]{4,3,2,1,0:T(8,128)(2,1)}, bf16[1,1,2,512,512]{4,3,2,1,0:T(8,128)(2,1)}) custom-call(bf16[1,1,2,512,512]{4,3,2,1,0:T(8,128)(2,1)S(1)} %get-tuple-element.11.less_new, bf16[2,512,512]{2,1,0:T(8,128)(2,1)S(1)} %get-tuple-element.12.ret_held, ...), custom_call_target="tpu_custom_call" | custom-call | flops 1073741824 | bytes 3145728 | tf_op jit(solution)/shard_map/pallas_call | solution.py:387
  (1 shorter events, 0.0 us)
Async XLA Ops:
  0.6 0.7 copy-start

commit v4 on v3

--- a/solution.py
+++ b/solution.py
@@ -2,6 +2,7 @@
 
 import jax
 import jax.numpy as jnp
+import numpy as np
 from jax import lax
 from jax.experimental import pallas as pl
 from jax.experimental.pallas import tpu as pltpu
@@ -342,13 +343,14 @@
     whole = pltpu.VMEM((2, order, order), jnp.bfloat16)
     new = jax.ShapeDtypeStruct(lesser.shape, jnp.bfloat16)
     total = jax.ShapeDtypeStruct((order, order), jnp.float32)
-    length = max(energies, momenta)
+    length = max(energies, momenta, modes)
     packed = (modes, momenta + 3, length)
-    row = lax.broadcasted_iota(jnp.int32, packed, 1)
-    grains = (lax.broadcast_in_dim(occupation, packed, (0,)) * GRAIN).astype(jnp.int32)
+    last = np.zeros(packed, np.float32)
+    last[:, momenta + 2] = GRAIN
+    phonons = lax.broadcast_in_dim(occupation, packed, (0,)) * last
     weights = lax.pad(coupling, 0, ((0, 0, 0), (0, 3, 0), (0, length - momenta, 0)))
     slots = lax.pad(shift_slots, 0, ((0, 0, 0), (momenta, 1, 0), (0, length - energies, 0)))
-    small = jnp.where(row == momenta + 2, grains, weights + slots)
+    small = weights + slots + phonons.astype(jnp.int32)
     held = pl.pallas_call(
         functools.partial(kernel, sizes, factor, widths, tail),
         out_shape=(

time: 99.7 us -> 99 us (level)
  no operation moved by 1% of the time
where the time goes in v4:
time: 99 us; the launch traced here: 98.8 us
  Pallas kernels  97.4 us (98%)
    pallas_call x1, Pallas kernels, per_device(): pl.pallas_call(functools.partial(kernel, sizes, factor, widths, tail), ou...  95.5 us

profile of v4, /device:TPU:9, one launch (start us, length us, event | category | flops | bytes accessed | tf_op | source)
XLA Modules:
  0.0 98.8 jit_solution(7169248941457064430)
XLA Ops:
  0.6 0.8 convert_add_fusion.small_ref
  1.4 95.5 %shard_map.94 = (bf16[1,1,2,512,512]{4,3,2,1,0:T(8,128)(2,1)S(1)}, bf16[2,512,512]{2,1,0:T(8,128)(2,1)S(1)}, f32[2,512,128]{2,1,0:T(8,128)S(1)}, bf16[2,512,128]...) custom-call(bf16[1,1,2,512,512]{4,3,2,1,0:T(8,128)(2,1)} %less_ref.1, ...), custom_call_target="tpu_custom_call" | custom-call | flops 5368709120 | bytes 6291456 | tf_op jit(solution)/shard_map/pallas_call | solution.py:354
  96.9 1.9 %shard_map.95 = (bf16[1,1,2,512,512]{4,3,2,1,0:T(8,128)(2,1)}, bf16[1,1,2,512,512]{4,3,2,1,0:T(8,128)(2,1)}, bf16[1,1,2,512,512]{4,3,2,1,0:T(8,128)(2,1)}) custom-call(bf16[1,1,2,512,512]{4,3,2,1,0:T(8,128)(2,1)S(1)} %get-tuple-element.11.less_new, bf16[2,512,512]{2,1,0:T(8,128)(2,1)S(1)} %get-tuple-element.12.ret_held, ...), custom_call_target="tpu_custom_call" | custom-call | flops 1073741824 | bytes 3145728 | tf_op jit(solution)/shard_map/pallas_call | solution.py:389

commit v5 on v4

--- a/solution.py
+++ b/solution.py
@@ -104,10 +104,14 @@
         skip = 0 if first else 1
         if skip:
             act((far_half + 1 - lax.rem(my_quarter, 2)) * quarter + lax.rem(me, quarter))
-        if "low" in which:
+        if len(which) == 2:
+            blend([far_half, far_half + 1], ending, skip)
+            blend([near_quarter], ending)
+            lax.fori_loop(0, quarter - 1, own, 0)
+        elif "low" in which:
             blend([far_half], ending, skip)
             blend([near_quarter], ending)
-        if "high" in which:
+        else:
             blend([far_half + 1], ending, skip)
             lax.fori_loop(0, quarter - 1, own, 0)
 

time: 99 us -> 98.9 us (level)
  no operation moved by 1% of the time
where the time goes in v5:
time: 98.9 us; the launch traced here: 98.7 us
  Pallas kernels  97.3 us (98%)
    pallas_call x1, Pallas kernels, per_device(): pl.pallas_call(functools.partial(kernel, sizes, factor, widths, tail), ou...  95.3 us

profile of v5, /device:TPU:9, one launch (start us, length us, event | category | flops | bytes accessed | tf_op | source)
XLA Modules:
  0.0 98.7 jit_solution(2301743999212444408)
XLA Ops:
  0.6 0.8 convert_add_fusion.small_ref
  1.4 95.3 %shard_map.94 = (bf16[1,1,2,512,512]{4,3,2,1,0:T(8,128)(2,1)S(1)}, bf16[2,512,512]{2,1,0:T(8,128)(2,1)S(1)}, f32[2,512,128]{2,1,0:T(8,128)S(1)}, bf16[2,512,128]...) custom-call(bf16[1,1,2,512,512]{4,3,2,1,0:T(8,128)(2,1)} %less_ref.1, ...), custom_call_target="tpu_custom_call" | custom-call | flops 5368709120 | bytes 6291456 | tf_op jit(solution)/shard_map/pallas_call | solution.py:358
  96.8 1.9 %shard_map.95 = (bf16[1,1,2,512,512]{4,3,2,1,0:T(8,128)(2,1)}, bf16[1,1,2,512,512]{4,3,2,1,0:T(8,128)(2,1)}, bf16[1,1,2,512,512]{4,3,2,1,0:T(8,128)(2,1)}) custom-call(bf16[1,1,2,512,512]{4,3,2,1,0:T(8,128)(2,1)S(1)} %get-tuple-element.11.less_new, bf16[2,512,512]{2,1,0:T(8,128)(2,1)S(1)} %get-tuple-element.12.ret_held, ...), custom_call_target="tpu_custom_call" | custom-call | flops 1073741824 | bytes 3145728 | tf_op jit(solution)/shard_map/pallas_call | solution.py:393
